TPU v7x, 32 devices: a whole 2x2x4 slice. The times are simulated.
32 devices in a mesh: dp: 32 (over z, y, x, core).
Axes of the slice: x: 2, y: 2, z: 4, core: 2. Of those that a mesh axis runs over, the one named last changes fastest.
Arguments:
- latents_in: bfloat16 [512, 256, 384], P('dp'), may hold values from -6 to 6
- class_ids: int32 [512], P('dp'), may hold values from 0 to 1000
- step_ids: int32 [512], P('dp'), may hold values from 0 to 999
- class_table: bfloat16 [1001, 384], replicated, may hold values from -4.1875 to 4.1875
- step_table: bfloat16 [1000, 384], replicated, may hold values from -4.1875 to 4.1875
- params: bfloat16 [2662400], P('dp'), may hold values from -1.5 to 1.5
- cotangent: bfloat16 [512, 256, 384], P('dp'), may hold values from -6 to 6
Outputs:
- block_out: bfloat16 [512, 256, 384], P('dp')
- grad_latents: bfloat16 [512, 256, 384], P('dp')
- grad_condition: float32 [512, 384], P('dp')
- grad_params: float32 [2662400], P('dp')
All inputs are finite; a program needn't handle non-finite values.
Results may differ from a plain program's by a relative error of at most 0.012.
The roundings to bfloat16 on the way count: a program that leaves them out, or rounds other values in their place, can miss the bound.
Values may be sent and summed in bfloat16 or wider, within the bound.
A program may use at most 192 MiB of HBM per device.

v0:
```python
from functools import partial
import math

import jax
import jax.numpy as jnp
from jax import lax
from jax.sharding import PartitionSpec as P

D = 384
HEADS = 6
HEAD_DIM = 64
FF = 1536
SEQ = 256
MICRO = 4


def carve(flat_params):
    shapes = (
        (D, 6 * D),
        (6 * D,),
        (D, 3 * D),
        (D,),
        (D,),
        (D, D),
        (D,),
        (D, FF),
        (FF,),
        (FF, D),
        (D,),
    )
    pieces = []
    offset = 0
    for extent in shapes:
        number = math.prod(extent)
        pieces.append(flat_params[offset : offset + number].reshape(extent))
        offset = offset + number
    return pieces


def pack(grads, padded):
    joined = jnp.concatenate([member.reshape(-1) for member in grads])
    return jnp.concatenate([joined, jnp.zeros((padded - joined.shape[0],), jnp.float32)])


def normalize(values):
    average = jnp.mean(values, axis=-1, keepdims=True)
    centered = values - average
    inv_std = lax.rsqrt(jnp.mean(centered * centered, axis=-1, keepdims=True) + 1e-06)
    return (centered * inv_std, inv_std)


def norm_back(grad_normed, normed, inv_std):
    mean_grad = jnp.mean(grad_normed, axis=-1, keepdims=True)
    mean_proj = jnp.mean(grad_normed * normed, axis=-1, keepdims=True)
    return inv_std * (grad_normed - mean_grad - normed * mean_proj)


def split_six(modulation):
    return [modulation[:, None, column * D : (column + 1) * D] for column in range(6)]


def run_forward(weights, block, silu_block):
    ada_w, ada_b, qkv_w, q_b, v_b, out_w, out_b, fc1_w, fc1_b, fc2_w, fc2_b = weights
    batch_count = block.shape[0]
    modulation = jnp.dot(silu_block, ada_w, preferred_element_type=jnp.float32) + ada_b.astype(
        jnp.float32
    )
    shift_a, scale_a, gate_a, shift_m, scale_m, gate_m = split_six(modulation)
    latents = block.astype(jnp.float32)
    normed_a, inv_a = normalize(latents)
    hidden_a = (normed_a * (1.0 + scale_a) + shift_a).astype(jnp.bfloat16).reshape(-1, D)
    qkv_bias = jnp.concatenate([q_b, jnp.zeros_like(q_b), v_b]).astype(jnp.float32)
    projected = (jnp.dot(hidden_a, qkv_w, preferred_element_type=jnp.float32) + qkv_bias).astype(
        jnp.bfloat16
    )
    heads_view = projected.reshape(batch_count, SEQ, 3, HEADS, HEAD_DIM)
    query_b, key_b, value_b = (heads_view[:, :, 0], heads_view[:, :, 1], heads_view[:, :, 2])
    scores = jnp.einsum(
        "lshd,lthd->lhst", query_b, key_b, preferred_element_type=jnp.float32
    ) * HEAD_DIM ** (-0.5)
    top_score = jnp.max(scores, axis=-1, keepdims=True)
    log_total = top_score + jnp.log(jnp.sum(jnp.exp(scores - top_score), axis=-1, keepdims=True))
    probs_b = jnp.exp(scores - log_total).astype(jnp.bfloat16)
    context = (
        jnp.einsum("lhst,lthd->lshd", probs_b, value_b, preferred_element_type=jnp.float32)
        .astype(jnp.bfloat16)
        .reshape(-1, D)
    )
    attended = (
        jnp.dot(context, out_w, preferred_element_type=jnp.float32) + out_b.astype(jnp.float32)
    ).reshape(batch_count, SEQ, D)
    resid_a = latents + gate_a * attended
    normed_m, inv_m = normalize(resid_a)
    hidden_m = (normed_m * (1.0 + scale_m) + shift_m).astype(jnp.bfloat16).reshape(-1, D)
    pre_act = jnp.dot(hidden_m, fc1_w, preferred_element_type=jnp.float32) + fc1_b.astype(
        jnp.float32
    )
    activated = jax.nn.gelu(pre_act, approximate=True).astype(jnp.bfloat16)
    mlp_out = (
        jnp.dot(activated, fc2_w, preferred_element_type=jnp.float32) + fc2_b.astype(jnp.float32)
    ).reshape(batch_count, SEQ, D)
    result = (resid_a + gate_m * mlp_out).astype(jnp.bfloat16)
    kept = (
        modulation,
        normed_a,
        inv_a,
        hidden_a,
        query_b,
        key_b,
        value_b,
        log_total,
        context,
        attended,
        normed_m,
        inv_m,
        hidden_m,
        pre_act,
        activated,
        mlp_out,
    )
    return (result, kept)


def run_backward(weights, kept, silu_block, condition, cot_block):
    ada_w, ada_b, qkv_w, q_b, v_b, out_w, out_b, fc1_w, fc1_b, fc2_w, fc2_b = weights
    (
        modulation,
        normed_a,
        inv_a,
        hidden_a,
        query_b,
        key_b,
        value_b,
        log_total,
        context,
        attended,
        normed_m,
        inv_m,
        hidden_m,
        pre_act,
        activated,
        mlp_out,
    ) = kept
    shift_a, scale_a, gate_a, shift_m, scale_m, gate_m = split_six(modulation)
    batch_count = cot_block.shape[0]
    grad_out = cot_block.astype(jnp.float32)
    grad_gate_m = jnp.sum(grad_out * mlp_out, axis=1)
    grad_mlp = (grad_out * gate_m).astype(jnp.bfloat16).reshape(-1, D)
    grad_fc2_w = jnp.einsum("ta,td->ad", activated, grad_mlp, preferred_element_type=jnp.float32)
    grad_fc2_b = jnp.sum(grad_mlp, axis=0, dtype=jnp.float32)
    grad_act = jnp.einsum("td,ad->ta", grad_mlp, fc2_w, preferred_element_type=jnp.float32)
    gelu_pull = jax.vjp(partial(jax.nn.gelu, approximate=True), pre_act)[1]
    grad_pre = gelu_pull(grad_act)[0].astype(jnp.bfloat16)
    grad_fc1_w = jnp.einsum("td,ta->da", hidden_m, grad_pre, preferred_element_type=jnp.float32)
    grad_fc1_b = jnp.sum(grad_pre, axis=0, dtype=jnp.float32)
    grad_hidden_m = jnp.einsum(
        "ta,da->td", grad_pre, fc1_w, preferred_element_type=jnp.float32
    ).reshape(batch_count, SEQ, D)
    grad_shift_m = jnp.sum(grad_hidden_m, axis=1)
    grad_scale_m = jnp.sum(grad_hidden_m * normed_m, axis=1)
    grad_resid = grad_out + norm_back(grad_hidden_m * (1.0 + scale_m), normed_m, inv_m)
    grad_gate_a = jnp.sum(grad_resid * attended, axis=1)
    grad_attn = (grad_resid * gate_a).astype(jnp.bfloat16).reshape(-1, D)
    grad_out_w = jnp.einsum("tc,td->cd", context, grad_attn, preferred_element_type=jnp.float32)
    grad_out_b = jnp.sum(grad_attn, axis=0, dtype=jnp.float32)
    grad_context = (
        jnp.einsum("td,cd->tc", grad_attn, out_w, preferred_element_type=jnp.float32)
        .astype(jnp.bfloat16)
        .reshape(batch_count, SEQ, HEADS, HEAD_DIM)
    )
    scale_factor = HEAD_DIM ** (-0.5)
    scores = (
        jnp.einsum("lshd,lthd->lhst", query_b, key_b, preferred_element_type=jnp.float32)
        * scale_factor
    )
    probs = jnp.exp(scores - log_total)
    grad_probs = jnp.einsum(
        "lshd,lthd->lhst", grad_context, value_b, preferred_element_type=jnp.float32
    )
    grad_value = jnp.einsum(
        "lhst,lshd->lthd",
        probs.astype(jnp.bfloat16),
        grad_context,
        preferred_element_type=jnp.float32,
    )
    weighted = jnp.sum(grad_probs * probs, axis=-1, keepdims=True)
    grad_scores = (probs * (grad_probs - weighted)).astype(jnp.bfloat16)
    grad_query = (
        jnp.einsum("lhst,lthd->lshd", grad_scores, key_b, preferred_element_type=jnp.float32)
        * scale_factor
    )
    grad_key = (
        jnp.einsum("lhst,lshd->lthd", grad_scores, query_b, preferred_element_type=jnp.float32)
        * scale_factor
    )
    grad_qkv = (
        jnp.stack([grad_query, grad_key, grad_value], axis=2)
        .astype(jnp.bfloat16)
        .reshape(-1, 3 * D)
    )
    grad_qkv_w = jnp.einsum("tc,tq->cq", hidden_a, grad_qkv, preferred_element_type=jnp.float32)
    bias_sums = jnp.sum(grad_qkv, axis=0, dtype=jnp.float32)
    grad_q_b = bias_sums[:D]
    grad_v_b = bias_sums[2 * D :]
    grad_hidden_a = jnp.einsum(
        "tq,cq->tc", grad_qkv, qkv_w, preferred_element_type=jnp.float32
    ).reshape(batch_count, SEQ, D)
    grad_shift_a = jnp.sum(grad_hidden_a, axis=1)
    grad_scale_a = jnp.sum(grad_hidden_a * normed_a, axis=1)
    grad_latent = (grad_resid + norm_back(grad_hidden_a * (1.0 + scale_a), normed_a, inv_a)).astype(
        jnp.bfloat16
    )
    grad_mod = jnp.concatenate(
        [grad_shift_a, grad_scale_a, grad_gate_a, grad_shift_m, grad_scale_m, grad_gate_m], axis=-1
    ).astype(jnp.bfloat16)
    grad_ada_w = jnp.einsum("lc,lm->cm", silu_block, grad_mod, preferred_element_type=jnp.float32)
    grad_ada_b = jnp.sum(grad_mod, axis=0, dtype=jnp.float32)
    grad_silu = jnp.einsum("lm,cm->lc", grad_mod, ada_w, preferred_element_type=jnp.float32)
    grad_cond = jax.vjp(jax.nn.silu, condition)[1](grad_silu)[0]
    grads = [
        grad_ada_w,
        grad_ada_b,
        grad_qkv_w,
        grad_q_b,
        grad_v_b,
        grad_out_w,
        grad_out_b,
        grad_fc1_w,
        grad_fc1_b,
        grad_fc2_w,
        grad_fc2_b,
    ]
    return (grads, grad_latent, grad_cond)


def on_device(latents_in, class_ids, step_ids, class_table, step_table, params, cotangent):
    padded = params.shape[0] * lax.axis_size("dp")
    micro_size = latents_in.shape[0] // MICRO
    class_hot = (
        class_ids[:, None] == jnp.arange(class_table.shape[0], dtype=jnp.int32)[None, :]
    ).astype(jnp.bfloat16)
    step_hot = (
        step_ids[:, None] == jnp.arange(step_table.shape[0], dtype=jnp.int32)[None, :]
    ).astype(jnp.bfloat16)
    condition = jnp.dot(class_hot, class_table, preferred_element_type=jnp.float32) + jnp.dot(
        step_hot, step_table, preferred_element_type=jnp.float32
    )
    silu_cond = jax.nn.silu(condition).astype(jnp.bfloat16)
    outputs = []
    grad_latents = []
    grad_conds = []
    running = None
    for micro_index in range(MICRO):
        first_row = micro_index * micro_size
        last_row = first_row + micro_size
        forward_weights = carve(lax.all_gather(params, "dp", axis=0, tiled=True))
        result, kept = run_forward(
            forward_weights, latents_in[first_row:last_row], silu_cond[first_row:last_row]
        )
        backward_weights = carve(lax.all_gather(params, "dp", axis=0, tiled=True))
        grads, grad_latent, grad_cond = run_backward(
            backward_weights,
            kept,
            silu_cond[first_row:last_row],
            condition[first_row:last_row],
            cotangent[first_row:last_row],
        )
        outputs.append(result)
        grad_latents.append(grad_latent)
        grad_conds.append(grad_cond)
        running = grads if running is None else jax.tree.map(jnp.add, running, grads)
    grad_params = lax.psum_scatter(pack(running, padded), "dp", scatter_dimension=0, tiled=True)
    return (
        jnp.concatenate(outputs, axis=0),
        jnp.concatenate(grad_latents, axis=0),
        jnp.concatenate(grad_conds, axis=0),
        grad_params,
    )


def solution(mesh):
    in_specs = (P("dp", None, None), P("dp"), P("dp"), P(), P(), P("dp"), P("dp", None, None))
    out_specs = (P("dp", None, None), P("dp", None, None), P("dp", None), P("dp"))
    return jax.shard_map(
        on_device, mesh=mesh, in_specs=in_specs, out_specs=out_specs, check_vma=False
    )
```

profile of v0, /device:TPU:0, one launch (start us, length us, event | category | flops | bytes accessed | tf_op | source)
XLA Modules:
  0.0 836.6 jit_solution(10781158005737942145)
XLA Ops:
  14.5 87.1 %all-gather.3.cloned.1.call-done = bf16[32,1,83200]{2,1,0:T(2,128)(2,1)} async-done(((bf16[1,1,83200]{2,1,0:T(2,128)(2,1)}), bf16[32,1,83200]{2,1,0:T(2,128)(2,1)}) %all-gather.3.cloned.1.call-update) | async-done | bytes 5324816 | tf_op jit(solution)/shard_map/all_gather | solution.py:256
  101.6 34.0 %reduce.12 = bf16[32,83200]{1,0:T(8,128)(2,1)} reduce(bf16[32,1,83200]{2,1,0:T(2,128)(2,1)} %all-gather.3.cloned.1.call-done, bf16[]{:T(256)} %constant.76), dimensions={1}, to_apply=%all-gather.reduce_sub_computation | reduce | bytes 10649602 | tf_op jit(solution)/shard_map/all_gather | solution.py:256
  135.6 10.4 %reshape.587 = bf16[2662400]{0:T(1024)(128)(2,1)} reshape(bf16[32,83200]{1,0:T(8,128)(2,1)} %reduce.12) | data formatting | bytes 10649600
  156.2 3.6 fusion.180
  159.8 3.6 reshape.540
  164.9 3.6 reshape.588
  175.9 4.0 fusion.32
  180.0 4.3 copy.167
  184.2 5.6 reshape.543
  205.8 3.3 fusion.200
  209.1 6.6 convert_reduce_fusion.3
  233.7 5.3 fusion.116
  247.7 3.4 copy.223
  254.3 4.4 fusion.94
  264.9 4.3 copy.179
  269.1 5.7 reshape.558
  274.9 3.9 fusion.182
  281.7 4.3 copy.173
  285.9 5.6 reshape.552
  291.5 3.8 fusion.181
  298.2 4.3 copy.185
  302.4 5.8 reshape.564
  349.1 6.7 convert_reduce_fusion.2
  355.9 6.0 multiply_reduce_fusion.12
  362.0 5.9 fusion.97
  371.0 6.6 convert_reduce_fusion.1
  377.6 6.6 convert_reduce_fusion
  390.4 3.7 convert_reduce_fusion.17
  397.5 5.1 fusion.119
  402.5 5.0 multiply_reduce_fusion
  413.3 3.4 copy.226
  420.8 5.2 fusion.117
  426.0 5.0 multiply_reduce_fusion.2
  436.8 3.4 copy.224
  444.5 5.1 fusion.118
  449.5 5.0 multiply_reduce_fusion.1
  460.6 3.5 copy.225
  473.1 3.3 convolution_add_fusion.15
  480.8 4.3 convolution_add_fusion.14
  497.1 4.7 fusion.193
  505.9 4.7 fusion.192
  520.7 7.4 fusion.85
  538.4 4.6 reshape.581
  542.9 4.1 constant_dynamic-update-slice_fusion.24
  548.4 16.3 %dynamic-update-slice.2 = f32[2662400]{0:T(1024)} dynamic-update-slice(f32[2662400]{0:T(1024)} %add_dynamic-update-slice_fusion, f32[442368]{0:T(1024)} %reshape.582, s32[]{} %constant.79) | dynamic-update-slice | bytes 3538948
  569.5 21.3 %dynamic-update-slice.7 = f32[2662400]{0:T(1024)} dynamic-update-slice(f32[2662400]{0:T(1024)} %constant_dynamic-update-slice_fusion.26, f32[589824]{0:T(1024)} %reshape.584, s32[]{} %constant.84) | dynamic-update-slice | bytes 4718596
  592.2 20.1 %dynamic-update-slice.9 = f32[2662400]{0:T(1024)} dynamic-update-slice(f32[2662400]{0:T(1024)} %add_dynamic-update-slice_fusion.1, f32[589824]{0:T(1024)S(1)} %reshape.585, s32[]{} %constant.86) | dynamic-update-slice | bytes 4718596
  624.4 203.3 %all-reduce.3.cloned.1.call-done = f32[2662400]{0:T(1024)} async-done(((f32[2662400]{0:T(1024)}), f32[2662400]{0:T(1024)}) %all-reduce.3.cloned.1.call-update) | async-done | bytes 10649616
  (603 shorter events, 233.1 us)
Async XLA Ops:
  7.2 6.2 copy-start
  7.2 6.2 copy-start.168
  7.2 94.4 %all-gather.3.cloned.1.call-start = ((), (), s32[]{:S(2)}) async-start(), calls=%async_computation | async-start | bytes 10982400 | tf_op jit(solution)/shard_map/all_gather | solution.py:256
  9.2 818.5 %all-reduce.3.cloned.1.call-start = ((), (), s32[]{:S(2)}) async-start(), calls=%async_computation.1 | async-start | bytes 21299200
  13.3 245.4 %copy-start.147 = (f32[4,256]{1,0:T(4,128)}, f32[4,256]{1,0:T(4,128)S(1)}, u32[]{:S(2)}) copy-start(f32[4,256]{1,0:T(4,128)S(1)} %get-tuple-element.203) | copy-start | bytes 12292
  13.4 245.4 %copy-start.141 = (f32[4,256]{1,0:T(4,128)}, f32[4,256]{1,0:T(4,128)S(1)}, u32[]{:S(2)}) copy-start(f32[4,256]{1,0:T(4,128)S(1)} %get-tuple-element.204) | copy-start | bytes 12292
  13.4 245.4 %copy-start.143 = (f32[4,256]{1,0:T(4,128)}, f32[4,256]{1,0:T(4,128)S(1)}, u32[]{:S(2)}) copy-start(f32[4,256]{1,0:T(4,128)S(1)} %get-tuple-element.205) | copy-start | bytes 12292
  14.5 149.9 %copy-start.124 = (bf16[16,384]{1,0:T(8,128)(2,1)}, bf16[16,384]{1,0:T(8,128)(2,1)S(1)}, u32[]{:S(2)}) copy-start(bf16[16,384]{1,0:T(8,128)(2,1)S(1)} %get-tuple-element.167) | copy-start | bytes 36868
  169.9 32.8 %copy-start.14 = (bf16[384,1536]{1,0:T(8,128)(2,1)}, bf16[384,1536]{1,0:T(8,128)(2,1)S(1)}, u32[]{:S(2)}) copy-start(bf16[384,1536]{1,0:T(8,128)(2,1)S(1)} %reshape.548) | copy-start | bytes 3538948
  172.8 42.9 %copy-start.75 = (bf16[1536,384]{1,0:T(8,128)(2,1)}, bf16[1536,384]{1,0:T(8,128)(2,1)S(1)}, u32[]{:S(2)}) copy-start(bf16[1536,384]{1,0:T(8,128)(2,1)S(1)} %reshape.549) | copy-start | bytes 3538948
  173.5 85.3 %copy-start.130 = (f32[4,384]{1,0:T(4,128)}, f32[4,384]{1,0:T(4,128)S(1)}, u32[]{:S(2)}) copy-start(f32[4,384]{1,0:T(4,128)S(1)} %get-tuple-element.155) | copy-start | bytes 18436
  222.6 36.2 %copy-start.132 = (f32[4,384]{1,0:T(4,128)}, f32[4,384]{1,0:T(4,128)S(1)}, u32[]{:S(2)}) copy-start(f32[4,384]{1,0:T(4,128)S(1)} %get-tuple-element.143) | copy-start | bytes 18436
  222.6 36.2 %copy-start.134 = (f32[4,384]{1,0:T(4,128)}, f32[4,384]{1,0:T(4,128)S(1)}, u32[]{:S(2)}) copy-start(f32[4,384]{1,0:T(4,128)S(1)} %get-tuple-element.207) | copy-start | bytes 18436
  227.2 11.9 %slice-start.6 = ((s8[6291456]{0:T(1024)(128)(4,1)}), s8[2097152]{0:T(1024)(128)(4,1)S(1)}, s32[]{:S(2)}) async-start(s8[6291456]{0:T(1024)(128)(4,1)} %bitcast.347), calls=%async_computation.8 | async-start | bytes 4194304
  317.2 14.0 %copy-start.19 = (f32[1024,384]{1,0:T(8,128)}, f32[1024,384]{1,0:T(8,128)S(1)}, u32[]{:S(2)}) copy-start(f32[1024,384]{1,0:T(8,128)S(1)} %convolution_add_fusion.20) | copy-start | bytes 4718596
  324.5 6.7 copy-start.21
  339.4 38.2 %copy-start.27 = (f32[1024,1536]{1,0:T(8,128)}, f32[1024,1536]{1,0:T(8,128)S(1)}, u32[]{:S(2)}) copy-start(f32[1024,1536]{1,0:T(8,128)S(1)} %fusion.191) | copy-start | bytes 18874372
  344.1 26.9 %copy-start.11 = (f32[1024,1536]{1,0:T(8,128)}, f32[1024,1536]{1,0:T(8,128)S(1)}, u32[]{:S(2)}) copy-start(f32[1024,1536]{1,0:T(8,128)S(1)} %fusion.190) | copy-start | bytes 18874372
  355.9 6.0 copy-start.77
  355.9 6.1 copy-start.13
  355.9 6.1 copy-start.73
  355.9 6.1 copy-start.150
  362.0 6.6 copy-start.125
  367.9 9.6 %copy-start.127 = (bf16[4,2304]{1,0:T(4,128)(2,1)}, bf16[4,2304]{1,0:T(4,128)(2,1)S(1)}, u32[]{:S(2)}) copy-start(bf16[4,2304]{1,0:T(4,128)(2,1)S(1)} %constant_dynamic-update-slice_fusion) | copy-start | bytes 55300
  371.0 6.6 copy-start.106
  377.6 9.7 %copy-start.81 = (bf16[1024,1536]{1,0:T(8,128)(2,1)}, bf16[1024,1536]{1,0:T(8,128)(2,1)S(1)}, u32[]{:S(2)}) copy-start(bf16[1024,1536]{1,0:T(8,128)(2,1)S(1)} %get-tuple-element.197) | copy-start | bytes 9437188
  377.6 6.6 copy-start.101
  397.5 10.1 %slice-start.4 = ((s8[6291456]{0:T(1024)(128)(4,1)}), s8[4194304]{0:T(1024)(128)(4,1)S(1)}, s32[]{:S(2)}) async-start(s8[6291456]{0:T(1024)(128)(4,1)} %bitcast.345), calls=%async_computation.6 | async-start | bytes 8388608
  420.8 10.2 %slice-start.2 = ((s8[6291456]{0:T(1024)(128)(4,1)}), s8[4194304]{0:T(1024)(128)(4,1)S(1)}, s32[]{:S(2)}) async-start(s8[6291456]{0:T(1024)(128)(4,1)} %bitcast.343), calls=%async_computation.4 | async-start | bytes 8388608
  444.5 10.0 %slice-start = ((s8[6291456]{0:T(1024)(128)(4,1)}), s8[4194304]{0:T(1024)(128)(4,1)S(1)}, s32[]{:S(2)}) async-start(s8[6291456]{0:T(1024)(128)(4,1)} %bitcast.341), calls=%async_computation.2 | async-start | bytes 8388608
  464.1 5.7 slice-start.13
  467.3 5.8 slice-start.8
  520.6 7.5 copy-start.10
  520.6 7.5 copy-start.20
  520.6 7.5 copy-start.70
  520.6 7.5 copy-start.97
  520.6 9.4 %copy-start.98 = (f32[4,256,384]{2,1,0:T(8,128)S(1)}, f32[4,256,384]{2,1,0:T(8,128)}, u32[]{:S(2)}) copy-start(f32[4,256,384]{2,1,0:T(8,128)} %fusion.192) | copy-start | bytes 4718596
  548.4 19.8 %copy-start.158 = (f32[384]{0:T(512)S(1)}, f32[384]{0:T(512)}, u32[]{:S(2)}) copy-start(f32[384]{0:T(512)} %get-tuple-element.93) | copy-start | bytes 4612
  548.4 19.8 %copy-start.165 = (f32[384]{0:T(512)S(1)}, f32[384]{0:T(512)}, u32[]{:S(2)}) copy-start(f32[384]{0:T(512)} %get-tuple-element.104) | copy-start | bytes 4612
  569.5 21.3 %copy-start.159 = (f32[1536]{0:T(1024)S(1)}, f32[1536]{0:T(1024)}, u32[]{:S(2)}) copy-start(f32[1536]{0:T(1024)} %get-tuple-element.198) | copy-start | bytes 18436
  569.5 21.3 %copy-start.160 = (f32[1536]{0:T(1024)S(1)}, f32[1536]{0:T(1024)}, u32[]{:S(2)}) copy-start(f32[1536]{0:T(1024)} %get-tuple-element.200) | copy-start | bytes 18436
  569.5 21.3 %copy-start.161 = (f32[1536]{0:T(1024)S(1)}, f32[1536]{0:T(1024)}, u32[]{:S(2)}) copy-start(f32[1536]{0:T(1024)} %get-tuple-element.196) | copy-start | bytes 18436
  569.5 21.4 %copy-start.162 = (f32[1536]{0:T(1024)S(1)}, f32[1536]{0:T(1024)}, u32[]{:S(2)}) copy-start(f32[1536]{0:T(1024)} %get-tuple-element.194) | copy-start | bytes 18436
  592.2 20.1 %copy-start.156 = (f32[384]{0:T(512)S(1)}, f32[384]{0:T(512)}, u32[]{:S(2)}) copy-start(f32[384]{0:T(512)} %get-tuple-element.53) | copy-start | bytes 4612
  592.2 20.1 %copy-start.157 = (f32[384]{0:T(512)S(1)}, f32[384]{0:T(512)}, u32[]{:S(2)}) copy-start(f32[384]{0:T(512)} %get-tuple-element.96) | copy-start | bytes 4612
  592.2 20.1 %copy-start.163 = (f32[384]{0:T(512)S(1)}, f32[384]{0:T(512)}, u32[]{:S(2)}) copy-start(f32[384]{0:T(512)} %get-tuple-element.55) | copy-start | bytes 4612
  592.2 20.1 %copy-start.164 = (f32[384]{0:T(512)S(1)}, f32[384]{0:T(512)}, u32[]{:S(2)}) copy-start(f32[384]{0:T(512)} %get-tuple-element.107) | copy-start | bytes 4612
  621.4 208.1 %copy-start.1 = (bf16[1001,384]{1,0:T(8,128)(2,1)S(1)}, bf16[1001,384]{1,0:T(8,128)(2,1)}, u32[]{:S(2)}) copy-start(bf16[1001,384]{1,0:T(8,128)(2,1)} %param.10) | copy-start | bytes 2306308
  (141 other events, 380.6 us)
Sparse Core Ops, SparseCore 0:
  11.6 89.9 all-gather.2
  615.1 212.5 all-reduce.2
where the time goes:
time: 845 us; the launch traced here: 837 us
  waiting for transfers between devices  290 us (34%)
  local copies, waits for them, and re-layouts  233 us (28%)
  matrix products  207 us (24%)
  other arithmetic  90.1 us (11%)
  between operations  16.7 us (2%)
    unnamed x3, waiting for transfers between devices  203 us
    unnamed x410, local copies, waits for them, and re-layouts  114 us
    all_gather x1, waiting for transfers between devices, on_device(): forward_weights = carve(lax.all_gather(params, 'dp', axis=0, tiled=True))  87.1 us
    all_gather x1, other arithmetic, on_device(): forward_weights = carve(lax.all_gather(params, 'dp', axis=0, tiled=True))  34 us
    dot_general x4, matrix products, run_backward(): jnp.einsum('td,ad->ta', grad_mlp, fc2_w, preferred_element_type=jnp.float32)  26.5 us
    reshape x4, local copies, waits for them, and re-layouts, run_forward(): heads_view = projected.reshape(batch_count, SEQ, 3, HEADS, HEAD_DIM)  22.7 us
    dot_general x4, matrix products, run_backward(): jnp.einsum('tq,cq->tc', grad_qkv, qkv_w, preferred_element_type=jnp.float32)  21.1 us
    dot_general x4, matrix products, run_backward(): jnp.einsum('lhst,lshd->lthd', probs.astype(jnp.bfloat16), grad_context, p...  20.7 us
  transfers between devices with their start and end apart: 2, of which 2 were waited for; matrix products, arithmetic and copies ran while one was open for 1% of the time, Pallas kernels for 0%

commit v1 on v0

v1 whole, which is shorter than its diff:
```python
from functools import partial
import math

import jax
import jax.numpy as jnp
from jax import lax
from jax.experimental import pallas as pl
from jax.experimental.pallas import tpu as pltpu
from jax.sharding import PartitionSpec as P

D = 384
HEADS = 6
HEAD_DIM = 64
FF = 1536
SEQ = 256
LANE = 128
CHUNK = 512
F32 = jnp.float32
BF16 = jnp.bfloat16
LOG2E = math.log2(math.e)
GELU_C = math.sqrt(2.0 / math.pi)

SHAPES = (
    ("ada_w", D, 6 * D),
    ("ada_b", 1, 6 * D),
    ("qkv_w", D, 3 * D),
    ("q_b", 1, D),
    ("v_b", 1, D),
    ("out_w", D, D),
    ("out_b", 1, D),
    ("fc1_w", D, FF),
    ("fc1_b", 1, FF),
    ("fc2_w", FF, D),
    ("fc2_b", 1, D),
)
PLACE = {}
USED = 0
for _name, _rows, _cols in SHAPES:
    PLACE[_name] = (USED, _rows, _cols // LANE)
    USED += _rows * _cols // LANE


def dot(a, b):
    return jnp.dot(a, b, preferred_element_type=F32)


def dot_nt(a, b):
    return lax.dot_general(a, b, (((1,), (1,)), ((), ())), preferred_element_type=F32)


def dot_tn(a, b):
    return lax.dot_general(a, b, (((0,), (0,)), ((), ())), preferred_element_type=F32)


def load_piece(flat, name, column):
    start, rows, width = PLACE[name]
    if rows == 1:
        return flat[start + column : start + column + 1, :]
    return flat[pl.ds(start + column, rows, stride=width), :]


def store_piece(flat, name, column, value):
    start, rows, width = PLACE[name]
    if rows == 1:
        flat[start + column : start + column + 1, :] = value
    else:
        flat[pl.ds(start + column, rows, stride=width), :] = value


def layer_norm(values):
    average = jnp.mean(values, axis=-1, keepdims=True)
    centered = values - average
    inv_std = lax.rsqrt(jnp.mean(centered * centered, axis=-1, keepdims=True) + 1e-06)
    return centered * inv_std, inv_std


def norm_back(grad, normed, inv_std):
    mean_grad = jnp.mean(grad, axis=-1, keepdims=True)
    mean_proj = jnp.mean(grad * normed, axis=-1, keepdims=True)
    return inv_std * (grad - mean_grad - normed * mean_proj)


def column_sum(values):
    return jnp.sum(values, axis=0, keepdims=True)


def block_kernel(
    steps,
    lat_ref,
    cot_ref,
    cond_ref,
    par_ref,
    out_ref,
    glat_ref,
    gcond_ref,
    flat_ref,
    ada_w,
    qkv_w,
    out_w,
    fc1_w,
    fc2_w,
    qkv_t,
    out_t,
    fc1_t,
    fc2_t,
    biases,
    mod_ref,
    gmod_ref,
    d_qkv,
    d_out,
    d_fc1,
    d_fc2t,
    d_qkvb,
    d_outb,
    d_fc1b,
    d_fc2b,
):
    step = pl.program_id(0)
    tall = par_ref.shape[0]

    @pl.when(step == 0)
    def _():
        flat_ref[...] = par_ref[...].astype(F32)
        for name, ref in (
            ("ada_w", ada_w),
            ("qkv_w", qkv_w),
            ("out_w", out_w),
            ("fc1_w", fc1_w),
            ("fc2_w", fc2_w),
        ):
            for column in range(PLACE[name][2]):
                ref[:, column * LANE : (column + 1) * LANE] = load_piece(
                    flat_ref, name, column
                ).astype(BF16)
        qkv_t[...] = qkv_w[...].T
        out_t[...] = out_w[...].T
        fc1_t[...] = fc1_w[...].T
        fc2_t[...] = fc2_w[...].T
        biases[...] = jnp.zeros_like(biases)
        for row, (name, first) in enumerate(
            (("ada_b", 0), ("q_b", 0), ("v_b", 2 * D), ("out_b", 0), ("fc1_b", 0), ("fc2_b", 0))
        ):
            row = (0, 1, 1, 2, 3, 4)[row]
            for column in range(PLACE[name][2]):
                left = first + column * LANE
                biases[row : row + 1, left : left + LANE] = load_piece(flat_ref, name, column)
        cond = cond_ref[...]
        silu = (cond * jax.nn.sigmoid(cond)).astype(BF16)
        mod_ref[...] = dot(silu, ada_w[...]) + biases[0:1, :]
        for ref in (d_qkv, d_out, d_fc1, d_fc2t, d_qkvb, d_outb, d_fc1b, d_fc2b):
            ref[...] = jnp.zeros_like(ref)

    mod = mod_ref[pl.ds(step, 1), :]
    shift_a, scale_a, gate_a, shift_m, scale_m, gate_m = [
        mod[:, n * D : (n + 1) * D] for n in range(6)
    ]
    x = lat_ref[0].astype(F32)
    cot = cot_ref[0].astype(F32)
    normed_a, inv_a = layer_norm(x)
    hidden_a = (normed_a * (1.0 + scale_a) + shift_a).astype(BF16)
    qkv = (dot(hidden_a, qkv_w[...]) + biases[1:2, : 3 * D]).astype(BF16)
    query = qkv[:, :D] * BF16(HEAD_DIM**-0.5)
    key = qkv[:, D : 2 * D]
    value = qkv[:, 2 * D :]
    key_t = key.T * BF16(HEAD_DIM**-0.5)
    value_t = value.T
    low_half = lax.broadcasted_iota(jnp.int32, (SEQ, LANE), 1) < HEAD_DIM
    zero = jnp.zeros((SEQ, LANE), BF16)

    def half(values, head):
        return jnp.where(low_half, values, zero) if head % 2 == 0 else jnp.where(low_half, zero, values)

    def pair(values, head):
        left = head // 2 * LANE
        return values[:, left : left + LANE]

    probs = []
    probs_b = []
    ctx_rows = []
    for head in range(HEADS):
        rows = slice(head * HEAD_DIM, (head + 1) * HEAD_DIM)
        scores = dot_nt(half(pair(key, head), head), pair(query, head)) * LOG2E
        grown = jnp.exp2(scores - jnp.max(scores, axis=0, keepdims=True))
        prob = grown * (1.0 / column_sum(grown))
        prob_b = prob.astype(BF16)
        probs.append(prob)
        probs_b.append(prob_b)
        ctx_rows.append(dot(value_t[rows, :], prob_b).astype(BF16))
    ctx_t = jnp.concatenate(ctx_rows, axis=0)
    attended = dot(ctx_t.T, out_w[...]) + biases[2:3, :D]
    resid = x + gate_a * attended
    normed_m, inv_m = layer_norm(resid)
    hidden_m = (normed_m * (1.0 + scale_m) + shift_m).astype(BF16)
    hidden_mt = hidden_m.T
    g_mlp = (cot * gate_m).astype(BF16)
    g_mlpt = g_mlp.T
    d_fc2b[...] += column_sum(g_mlp.astype(F32))
    mlp_out = biases[4:5, :D]
    g_hidden_m = None
    for left in range(0, FF, CHUNK):
        cols = slice(left, left + CHUNK)
        pre = dot(hidden_m, fc1_w[:, cols]) + biases[3:4, cols]
        square = pre * pre
        gate = 0.5 + 0.5 * jnp.tanh(pre * (GELU_C + (GELU_C * 0.044715) * square))
        act = pre * gate
        slope = gate + act * (1.0 - gate) * (2.0 * GELU_C + (6.0 * GELU_C * 0.044715) * square)
        act_b = act.astype(BF16)
        mlp_out = mlp_out + dot(act_b, fc2_w[cols, :])
        g_pre = dot(g_mlp, fc2_t[:, cols]) * slope
        g_pre_b = g_pre.astype(BF16)
        part = dot(g_pre_b, fc1_t[cols, :])
        g_hidden_m = part if g_hidden_m is None else g_hidden_m + part
        d_fc2t[:, cols] += dot(g_mlpt, act_b)
        d_fc1[:, cols] += dot(hidden_mt, g_pre_b)
        d_fc1b[:, cols] += column_sum(g_pre_b.astype(F32))
    out_ref[0] = (resid + gate_m * mlp_out).astype(BF16)
    g_gate_m = column_sum(cot * mlp_out)
    g_shift_m = column_sum(g_hidden_m)
    g_scale_m = column_sum(g_hidden_m * normed_m)
    g_resid = cot + norm_back(g_hidden_m * (1.0 + scale_m), normed_m, inv_m)
    g_gate_a = column_sum(g_resid * attended)
    g_attn = (g_resid * gate_a).astype(BF16)
    d_out[...] += dot(ctx_t, g_attn)
    d_outb[...] += column_sum(g_attn.astype(F32))
    g_ctx = dot(g_attn, out_t[...]).astype(BF16)
    gq_rows = []
    g_keys = []
    g_values = []
    for head in range(HEADS):
        rows = slice(head * HEAD_DIM, (head + 1) * HEAD_DIM)
        g_prob = dot_nt(half(pair(value, head), head), pair(g_ctx, head))
        prob = probs[head]
        g_score = (prob * (g_prob - column_sum(g_prob * prob))).astype(BF16)
        gq_rows.append(dot(key_t[rows, :], g_score).astype(BF16))
        g_key = dot(g_score, pair(query, head))
        g_value = dot(probs_b[head], pair(g_ctx, head))
        if head % 2 == 0:
            even = (g_key, g_value)
        else:
            g_keys.append(jnp.where(low_half, even[0], g_key).astype(BF16))
            g_values.append(jnp.where(low_half, even[1], g_value).astype(BF16))
    g_query = jnp.concatenate(gq_rows, axis=0).T
    g_qkv = jnp.concatenate([g_query] + g_keys + g_values, axis=1)
    d_qkv[...] += dot(hidden_a.T, g_qkv)
    d_qkvb[...] += column_sum(g_qkv.astype(F32))
    g_hidden_a = dot(g_qkv, qkv_t[...])
    g_shift_a = column_sum(g_hidden_a)
    g_scale_a = column_sum(g_hidden_a * normed_a)
    glat_ref[0] = (
        g_resid + norm_back(g_hidden_a * (1.0 + scale_a), normed_a, inv_a)
    ).astype(BF16)
    gmod_ref[pl.ds(step, 1), :] = jnp.concatenate(
        [g_shift_a, g_scale_a, g_gate_a, g_shift_m, g_scale_m, g_gate_m], axis=1
    )

    @pl.when(step == steps - 1)
    def _():
        cond = cond_ref[...]
        sig = jax.nn.sigmoid(cond)
        silu = (cond * sig).astype(BF16)
        g_mod = gmod_ref[...].astype(BF16)
        gcond_ref[...] = dot_nt(g_mod, ada_w[...]) * (sig * (1.0 + cond * (1.0 - sig)))
        mod_sum = column_sum(g_mod.astype(F32))

        def put(name, value, first=0):
            for column in range(PLACE[name][2]):
                left = first + column * LANE
                store_piece(flat_ref, name, column, value[:, left : left + LANE])

        for column in range(0, 6 * D, D):
            part = dot_tn(silu, g_mod[:, column : column + D])
            for inner in range(D // LANE):
                store_piece(
                    flat_ref,
                    "ada_w",
                    column // LANE + inner,
                    part[:, inner * LANE : (inner + 1) * LANE],
                )
        put("ada_b", mod_sum)
        put("qkv_w", d_qkv)
        put("q_b", d_qkvb)
        put("v_b", d_qkvb, 2 * D)
        put("out_w", d_out)
        put("out_b", d_outb)
        put("fc1_w", d_fc1)
        put("fc1_b", d_fc1b)
        for column in range(D // LANE):
            store_piece(
                flat_ref, "fc2_w", column, d_fc2t[column * LANE : (column + 1) * LANE, :].T
            )
        put("fc2_b", d_fc2b)
        flat_ref[USED:tall, :] = jnp.zeros((tall - USED, LANE), F32)


def run_block(latents, cotangent, condition, flat):
    count = latents.shape[0]
    tall = flat.shape[0]
    once = pl.Buffered(1)
    latent_spec = pl.BlockSpec((1, SEQ, D), lambda i: (i, 0, 0))
    return pl.pallas_call(
        partial(block_kernel, count),
        grid=(count,),
        in_specs=[
            latent_spec,
            latent_spec,
            pl.BlockSpec((count, D), lambda i: (0, 0), pipeline_mode=once),
            pl.BlockSpec((tall, LANE), lambda i: (0, 0), pipeline_mode=once),
        ],
        out_specs=[
            latent_spec,
            latent_spec,
            pl.BlockSpec((count, D), lambda i: (0, 0), pipeline_mode=once),
            pl.BlockSpec((tall, LANE), lambda i: (0, 0), pipeline_mode=once),
        ],
        out_shape=[
            jax.ShapeDtypeStruct(latents.shape, BF16),
            jax.ShapeDtypeStruct(latents.shape, BF16),
            jax.ShapeDtypeStruct((count, D), F32),
            jax.ShapeDtypeStruct((tall, LANE), F32),
        ],
        scratch_shapes=[
            pltpu.VMEM((D, 6 * D), BF16),
            pltpu.VMEM((D, 3 * D), BF16),
            pltpu.VMEM((D, D), BF16),
            pltpu.VMEM((D, FF), BF16),
            pltpu.VMEM((FF, D), BF16),
            pltpu.VMEM((3 * D, D), BF16),
            pltpu.VMEM((D, D), BF16),
            pltpu.VMEM((FF, D), BF16),
            pltpu.VMEM((D, FF), BF16),
            pltpu.VMEM((8, 6 * D), F32),
            pltpu.VMEM((count, 6 * D), F32),
            pltpu.VMEM((count, 6 * D), F32),
            pltpu.VMEM((D, 3 * D), F32),
            pltpu.VMEM((D, D), F32),
            pltpu.VMEM((D, FF), F32),
            pltpu.VMEM((D, FF), F32),
            pltpu.VMEM((1, 3 * D), F32),
            pltpu.VMEM((1, D), F32),
            pltpu.VMEM((1, FF), F32),
            pltpu.VMEM((1, D), F32),
        ],
        compiler_params=pltpu.CompilerParams(
            dimension_semantics=("arbitrary",), vmem_limit_bytes=60 * 1024 * 1024
        ),
    )(latents, cotangent, condition, flat)


def on_device(latents_in, class_ids, step_ids, class_table, step_table, params, cotangent):
    flat = lax.all_gather(params.reshape(-1, LANE), "dp", axis=0, tiled=True)
    class_hot = (
        class_ids[:, None] == jnp.arange(class_table.shape[0], dtype=jnp.int32)[None, :]
    ).astype(BF16)
    step_hot = (
        step_ids[:, None] == jnp.arange(step_table.shape[0], dtype=jnp.int32)[None, :]
    ).astype(BF16)
    condition = dot(class_hot, class_table) + dot(step_hot, step_table)
    block_out, grad_latents, grad_condition, grad_flat = run_block(
        latents_in, cotangent, condition, flat
    )
    grad_params = lax.psum_scatter(grad_flat, "dp", scatter_dimension=0, tiled=True)
    return block_out, grad_latents, grad_condition, grad_params.reshape(-1)


def solution(mesh):
    in_specs = (P("dp", None, None), P("dp"), P("dp"), P(), P(), P("dp"), P("dp", None, None))
    out_specs = (P("dp", None, None), P("dp", None, None), P("dp", None), P("dp"))
    return jax.shard_map(
        on_device, mesh=mesh, in_specs=in_specs, out_specs=out_specs, check_vma=False
    )
```

time: 845 us -> 389 us (0.46)
  local copies, waits for them, and re-layouts: 233 us -> 9.7 us
  waiting for transfers between devices: 290 us -> 69.8 us
  matrix products: 207 us -> 2.94 us
  Pallas kernels: 0 us -> 166 us
  blocking collectives: 0 us -> 120 us
  other arithmetic: 90.1 us -> 0 us
    dot_general x86 -> x2, matrix products: 207 us -> 2.94 us  [dot(): return jnp.dot(a, b, preferred_element_type=F32)]
    unnamed x3 -> x2, waiting for transfers between devices: 203 us -> 1.6 us
    pallas_call x0 -> x1, Pallas kernels: none -> 166 us  [run_block(): pl.pallas_call(partial(block_kernel, count), grid=(count,), in_specs=[lat...]
    unnamed x0 -> x1, blocking collectives: none -> 120 us
    unnamed x410 -> x5, local copies, waits for them, and re-layouts: 114 us -> 8.94 us
    reshape x20 -> x1, local copies, waits for them, and re-layouts: 54.7 us -> 0.76 us  [on_device(): return (block_out, grad_latents, grad_condition, grad_params.reshape(-1))]
    all_gather x1 -> x0, other arithmetic: 34 us -> none  [on_device(): forward_weights = carve(lax.all_gather(params, 'dp', axis=0, tiled=True))]
    reduce_sum x25 -> x0, other arithmetic: 27.2 us -> none  [the longest x3 5.74 us: normalize(): average = jnp.mean(values, axis=-1, keepdims=True)]
where the time goes in v1:
time: 389 us; the launch traced here: 384 us
  Pallas kernels  166 us (43%)
  blocking collectives  120 us (31%)
  waiting for transfers between devices  69.8 us (18%)
  between operations  14.1 us (4%)
  local copies, waits for them, and re-layouts  9.7 us (2%)
    pallas_call x1, Pallas kernels, run_block(): pl.pallas_call(partial(block_kernel, count), grid=(count,), in_specs=[lat...  166 us
    unnamed x1, blocking collectives  120 us
    all_gather x1, waiting for transfers between devices, on_device(): flat = lax.all_gather(params.reshape(-1, LANE), 'dp', axis=0, tiled=True)  68.2 us
    unnamed x5, local copies, waits for them, and re-layouts  8.94 us
  transfers between devices with their start and end apart: 2, of which 2 were waited for; matrix products, arithmetic and copies ran while one was open for 1% of the time, Pallas kernels for 0%

profile of v1, /device:TPU:0, one launch (start us, length us, event | category | flops | bytes accessed | tf_op | source)
XLA Modules:
  0.0 383.9 jit_solution(522928060722891878)
XLA Ops:
  7.2 0.0 copy-start
  7.2 0.0 all-gather.3.cloned.1.call-start
  7.2 0.7 all-gather.3.cloned.1.call-update
  7.9 0.4 copy-done
  8.3 0.9 fusion.1
  9.2 2.0 convolution_add_fusion.cond_ref
  11.2 68.2 %all-gather.3.cloned.1.call-done = bf16[32,650,128]{2,1,0:T(8,128)(2,1)} async-done(((bf16[1,650,128]{2,1,0:T(8,128)(2,1)}), bf16[32,650,128]{2,1,0:T(8,128)(2,1)}) %all-gather.3.cloned.1.call-update) | async-done | bytes 5324816 | tf_op jit(solution)/shard_map/all_gather | solution.py:350
  79.4 7.7 %reshape.19.par_ref = bf16[20800,128]{1,0:T(8,128)(2,1)} reshape(bf16[32,650,128]{2,1,0:T(8,128)(2,1)} %all-gather.3.cloned.1.call-done) | data formatting | bytes 10649600
  87.1 165.9 %shard_map.102 = (bf16[16,256,384]{2,1,0:T(8,128)(2,1)}, bf16[16,256,384]{2,1,0:T(8,128)(2,1)}, f32[16,384]{1,0:T(8,128)}, f32[20800,128]{1,0:T(8,128)}) custom-call(bf16[16,256,384]{2,1,0:T(8,128)(2,1)} %lat_ref.1, bf16[16,256,384]{2,1,0:T(8,128)(2,1)} %cot_ref.1, f32[16,384]{1,0:T(8,128)} %convolution_add_fusion.cond_ref, bf16[20800,128]{1,0:T(8,128)(2,1)} %reshape.19.par_ref), custom_call_target="tpu_custom_call" | custom-call | tf_op jit(solution)/shard_map/pallas_call | solution.py:300
  253.0 120.2 %fusion = f32[656,128]{1,0:T(8,128)S(1)} fusion(f32[20800,128]{1,0:T(8,128)} %get-tuple-element.11), kind=kCustom, calls=%all-reduce-scatter | all-reduce-scatter fusion | flops 2686977 | bytes 10985472
  373.2 1.4 collective-permute-start
  374.5 0.9 collective-permute-done
  375.4 0.8 concatenate
  376.3 0.8 dynamic-slice_bitcast_fusion
  (1 shorter events, 0.0 us)
Async XLA Ops:
  7.2 1.1 copy-start
  7.2 72.2 %all-gather.3.cloned.1.call-start = ((), (), s32[]{:S(2)}) async-start(), calls=%async_computation | async-start | bytes 5541888 | tf_op jit(solution)/shard_map/all_gather | solution.py:350
  373.2 2.3 collective-permute-start
Sparse Core Ops, SparseCore 0:
  10.8 68.5 all-gather.2

commit v2 on v1

--- a/solution.py
+++ b/solution.py
@@ -15,6 +15,7 @@
 SEQ = 256
 LANE = 128
 CHUNK = 512
+PER = 2
 F32 = jnp.float32
 BF16 = jnp.bfloat16
 LOG2E = math.log2(math.e)
@@ -40,6 +41,189 @@
     USED += _rows * _cols // LANE
 
 
+def bit_orders(count):
+    bits = list(range(count.bit_length() - 1))
+    return bits, bits[:1] + bits[2:3] + bits[1:2] + bits[3:]
+
+
+def place_of(owner, order):
+    place = 0
+    for bit in order:
+        place = place * 2 + owner // 2**bit % 2
+    return place
+
+
+def partner_of(me, bit):
+    return me + (1 - 2 * (me // 2**bit % 2)) * 2**bit
+
+
+def greet(me, bits):
+    barrier = pltpu.get_barrier_semaphore()
+    for bit in range(bits):
+        pl.semaphore_signal(
+            barrier,
+            inc=1,
+            device_id=(partner_of(me, bit),),
+            device_id_type=pl.DeviceIdType.MESH,
+        )
+    pl.semaphore_wait(barrier, bits)
+
+
+def gather_kernel(count, mine_ref, all_ref, own_sem, send_sem, recv_sem, hand_send, hand_recv):
+    me = lax.axis_index("dp")
+    orders = bit_orders(count)
+    bits = len(orders[0])
+    places = [place_of(me, order) for order in orders]
+    own = [
+        pltpu.make_async_copy(mine_ref.at[lane], all_ref.at[lane, places[lane]], own_sem.at[lane])
+        for lane in range(2)
+    ]
+    for copy in own:
+        copy.start()
+    greet(me, bits)
+
+    def start(lane, stage):
+        size = 2**stage
+        held = all_ref.at[lane, pl.ds(places[lane] // size * size, size)]
+        copy = pltpu.make_async_remote_copy(
+            src_ref=held,
+            dst_ref=held,
+            send_sem=send_sem.at[lane, stage],
+            recv_sem=recv_sem.at[lane, stage],
+            device_id=(partner_of(me, orders[lane][bits - 1 - stage]),),
+            device_id_type=pl.DeviceIdType.MESH,
+        )
+        copy.start()
+        return copy
+
+    def hand_over(lane, stage):
+        size = 1 if stage == 0 else 2 ** (stage - 1)
+        first = places[lane] // size
+        if stage > 0:
+            first = first + 1 - 2 * (first % 2)
+        held = all_ref.at[lane, pl.ds(first * size, size)]
+        copy = pltpu.make_async_remote_copy(
+            src_ref=held,
+            dst_ref=held,
+            send_sem=hand_send.at[lane, stage],
+            recv_sem=hand_recv.at[lane, stage],
+            device_id=(partner_of(me, 0),),
+            device_id_type=pl.DeviceIdType.MESH,
+        )
+        copy.start()
+        return copy
+
+    flying = []
+    handed = []
+    for lane in range(2):
+        own[lane].wait()
+        flying.append(start(lane, 0))
+        handed.append(hand_over(lane, 0))
+    for stage in range(1, bits):
+        for lane in range(2):
+            flying[lane].wait()
+            if stage < bits - 1:
+                flying[lane] = start(lane, stage)
+            handed.append(hand_over(lane, stage))
+    for copy in handed:
+        copy.wait()
+
+
+def gather(mine, count):
+    lanes, half, width = mine.shape
+    bits = count.bit_length() - 1
+    return pl.pallas_call(
+        partial(gather_kernel, count),
+        in_specs=[pl.BlockSpec(memory_space=pltpu.VMEM)],
+        out_specs=pl.BlockSpec(memory_space=pltpu.VMEM),
+        out_shape=jax.ShapeDtypeStruct((lanes, count, half, width), mine.dtype),
+        scratch_shapes=[
+            pltpu.SemaphoreType.DMA((2,)),
+            pltpu.SemaphoreType.DMA((2, bits)),
+            pltpu.SemaphoreType.DMA((2, bits)),
+            pltpu.SemaphoreType.DMA((2, bits)),
+            pltpu.SemaphoreType.DMA((2, bits)),
+        ],
+        compiler_params=pltpu.CompilerParams(
+            collective_id=0, has_side_effects=True, vmem_limit_bytes=40 * 1024 * 1024
+        ),
+    )(mine)
+
+
+def reduce_kernel(count, all_ref, sum_ref, land_ref, send_sem, recv_sem):
+    me = lax.axis_index("dp")
+    orders = bit_orders(count)
+    bits = len(orders[0])
+    places = [place_of(me, order) for order in orders]
+    greet(me, bits)
+
+    def start(lane, stage):
+        size = count // 2 ** (stage + 1)
+        side = places[lane] // size % 2
+        if stage == 0:
+            source = all_ref.at[lane, pl.ds((1 - side) * size, size)]
+        else:
+            source = land_ref.at[lane, pl.ds(2 * size + (1 - side) * size, size)]
+        copy = pltpu.make_async_remote_copy(
+            src_ref=source,
+            dst_ref=land_ref.at[lane, pl.ds(size, size)],
+            send_sem=send_sem.at[lane, stage],
+            recv_sem=recv_sem.at[lane, stage],
+            device_id=(partner_of(me, orders[lane][stage]),),
+            device_id_type=pl.DeviceIdType.MESH,
+        )
+        copy.start()
+        return copy
+
+    def add(lane, stage):
+        size = count // 2 ** (stage + 1)
+        side = places[lane] // size % 2
+
+        def one(block):
+            if stage == 0:
+                kept = all_ref[lane, side * size + block]
+            else:
+                kept = land_ref[lane, 2 * size + side * size + block]
+            return kept.astype(F32) + land_ref[lane, size + block].astype(F32)
+
+        if stage == bits - 1:
+            sum_ref[lane] = one(0)
+        else:
+
+            def body(block, carry):
+                land_ref[lane, size + block] = one(block).astype(BF16)
+                return carry
+
+            lax.fori_loop(0, size, body, 0)
+
+    flying = [start(lane, 0) for lane in range(2)]
+    for stage in range(bits):
+        for lane in range(2):
+            flying[lane].wait()
+            add(lane, stage)
+            if stage < bits - 1:
+                flying[lane] = start(lane, stage + 1)
+
+
+def reduce(parts):
+    lanes, count, half, width = parts.shape
+    bits = count.bit_length() - 1
+    return pl.pallas_call(
+        partial(reduce_kernel, count),
+        in_specs=[pl.BlockSpec(memory_space=pltpu.VMEM)],
+        out_specs=pl.BlockSpec(memory_space=pltpu.VMEM),
+        out_shape=jax.ShapeDtypeStruct((lanes, half, width), F32),
+        scratch_shapes=[
+            pltpu.VMEM((lanes, count, half, width), BF16),
+            pltpu.SemaphoreType.DMA((2, bits)),
+            pltpu.SemaphoreType.DMA((2, bits)),
+        ],
+        compiler_params=pltpu.CompilerParams(
+            collective_id=1, has_side_effects=True, vmem_limit_bytes=40 * 1024 * 1024
+        ),
+    )(parts)
+
+
 def dot(a, b):
     return jnp.dot(a, b, preferred_element_type=F32)
 
@@ -86,6 +270,7 @@
 
 def block_kernel(
     steps,
+    rows,
     lat_ref,
     cot_ref,
     cond_ref,
@@ -93,6 +278,7 @@
     out_ref,
     glat_ref,
     gcond_ref,
+    gpar_ref,
     flat_ref,
     ada_w,
     qkv_w,
@@ -116,11 +302,18 @@
     d_fc2b,
 ):
     step = pl.program_id(0)
-    tall = par_ref.shape[0]
+    owners, half_rows = par_ref.shape[1:3]
+    tall = owners * rows
+    orders = bit_orders(owners)
+    spans = ((0, half_rows), (half_rows, rows))
 
     @pl.when(step == 0)
     def _():
-        flat_ref[...] = par_ref[...].astype(F32)
+        for owner in range(owners):
+            for lane, (first, last) in enumerate(spans):
+                flat_ref[owner * rows + first : owner * rows + last, :] = par_ref[
+                    lane, place_of(owner, orders[lane])
+                ].astype(F32)[: last - first]
         for name, ref in (
             ("ada_w", ada_w),
             ("qkv_w", qkv_w),
@@ -150,20 +343,18 @@
         for ref in (d_qkv, d_out, d_fc1, d_fc2t, d_qkvb, d_outb, d_fc1b, d_fc2b):
             ref[...] = jnp.zeros_like(ref)
 
-    mod = mod_ref[pl.ds(step, 1), :]
+    each = range(PER)
+    mods = [mod_ref[pl.ds(step * PER + n, 1), :] for n in each]
     shift_a, scale_a, gate_a, shift_m, scale_m, gate_m = [
-        mod[:, n * D : (n + 1) * D] for n in range(6)
+        [mods[n][:, piece * D : (piece + 1) * D] for n in each] for piece in range(6)
     ]
-    x = lat_ref[0].astype(F32)
-    cot = cot_ref[0].astype(F32)
-    normed_a, inv_a = layer_norm(x)
-    hidden_a = (normed_a * (1.0 + scale_a) + shift_a).astype(BF16)
-    qkv = (dot(hidden_a, qkv_w[...]) + biases[1:2, : 3 * D]).astype(BF16)
-    query = qkv[:, :D] * BF16(HEAD_DIM**-0.5)
-    key = qkv[:, D : 2 * D]
-    value = qkv[:, 2 * D :]
-    key_t = key.T * BF16(HEAD_DIM**-0.5)
-    value_t = value.T
+
+    def join(parts):
+        return jnp.concatenate(parts, axis=0)
+
+    def cut(values):
+        return [values[n * SEQ : (n + 1) * SEQ] for n in each]
+
     low_half = lax.broadcasted_iota(jnp.int32, (SEQ, LANE), 1) < HEAD_DIM
     zero = jnp.zeros((SEQ, LANE), BF16)
 
@@ -174,25 +365,40 @@
         left = head // 2 * LANE
         return values[:, left : left + LANE]
 
-    probs = []
-    probs_b = []
-    ctx_rows = []
+    x = [lat_ref[n].astype(F32) for n in each]
+    cot = [cot_ref[n].astype(F32) for n in each]
+    normed_a, inv_a = zip(*[layer_norm(x[n]) for n in each])
+    hidden_a = join(
+        [(normed_a[n] * (1.0 + scale_a[n]) + shift_a[n]).astype(BF16) for n in each]
+    )
+    qkv = (dot(hidden_a, qkv_w[...]) + biases[1:2, : 3 * D]).astype(BF16)
+    query = cut(qkv[:, :D] * BF16(HEAD_DIM**-0.5))
+    key = cut(qkv[:, D : 2 * D])
+    value = cut(qkv[:, 2 * D :])
+    key_t = [key[n].T * BF16(HEAD_DIM**-0.5) for n in each]
+    value_t = [value[n].T for n in each]
+    probs = [[] for n in each]
+    probs_b = [[] for n in each]
+    ctx_rows = [[] for n in each]
     for head in range(HEADS):
-        rows = slice(head * HEAD_DIM, (head + 1) * HEAD_DIM)
-        scores = dot_nt(half(pair(key, head), head), pair(query, head)) * LOG2E
-        grown = jnp.exp2(scores - jnp.max(scores, axis=0, keepdims=True))
-        prob = grown * (1.0 / column_sum(grown))
-        prob_b = prob.astype(BF16)
-        probs.append(prob)
-        probs_b.append(prob_b)
-        ctx_rows.append(dot(value_t[rows, :], prob_b).astype(BF16))
-    ctx_t = jnp.concatenate(ctx_rows, axis=0)
-    attended = dot(ctx_t.T, out_w[...]) + biases[2:3, :D]
-    resid = x + gate_a * attended
-    normed_m, inv_m = layer_norm(resid)
-    hidden_m = (normed_m * (1.0 + scale_m) + shift_m).astype(BF16)
+        head_rows = slice(head * HEAD_DIM, (head + 1) * HEAD_DIM)
+        for n in each:
+            scores = dot_nt(half(pair(key[n], head), head), pair(query[n], head)) * LOG2E
+            grown = jnp.exp2(scores - jnp.max(scores, axis=0, keepdims=True))
+            prob = grown * (1.0 / column_sum(grown))
+            prob_b = prob.astype(BF16)
+            probs[n].append(prob)
+            probs_b[n].append(prob_b)
+            ctx_rows[n].append(dot(value_t[n][head_rows, :], prob_b).astype(BF16))
+    ctx_t = jnp.concatenate([join(ctx_rows[n]) for n in each], axis=1)
+    attended = cut(dot(ctx_t.T, out_w[...]) + biases[2:3, :D])
+    resid = [x[n] + gate_a[n] * attended[n] for n in each]
+    normed_m, inv_m = zip(*[layer_norm(resid[n]) for n in each])
+    hidden_m = join(
+        [(normed_m[n] * (1.0 + scale_m[n]) + shift_m[n]).astype(BF16) for n in each]
+    )
     hidden_mt = hidden_m.T
-    g_mlp = (cot * gate_m).astype(BF16)
+    g_mlp = join([(cot[n] * gate_m[n]).astype(BF16) for n in each])
     g_mlpt = g_mlp.T
     d_fc2b[...] += column_sum(g_mlp.astype(F32))
     mlp_out = biases[4:5, :D]
@@ -213,45 +419,62 @@
         d_fc2t[:, cols] += dot(g_mlpt, act_b)
         d_fc1[:, cols] += dot(hidden_mt, g_pre_b)
         d_fc1b[:, cols] += column_sum(g_pre_b.astype(F32))
-    out_ref[0] = (resid + gate_m * mlp_out).astype(BF16)
-    g_gate_m = column_sum(cot * mlp_out)
-    g_shift_m = column_sum(g_hidden_m)
-    g_scale_m = column_sum(g_hidden_m * normed_m)
-    g_resid = cot + norm_back(g_hidden_m * (1.0 + scale_m), normed_m, inv_m)
-    g_gate_a = column_sum(g_resid * attended)
-    g_attn = (g_resid * gate_a).astype(BF16)
+    mlp_out = cut(mlp_out)
+    g_hidden_m = cut(g_hidden_m)
+    g_resid = []
+    for n in each:
+        out_ref[n] = (resid[n] + gate_m[n] * mlp_out[n]).astype(BF16)
+        g_resid.append(
+            cot[n] + norm_back(g_hidden_m[n] * (1.0 + scale_m[n]), normed_m[n], inv_m[n])
+        )
+    late_mod = [
+        [
+            column_sum(g_resid[n] * attended[n]),
+            column_sum(g_hidden_m[n]),
+            column_sum(g_hidden_m[n] * normed_m[n]),
+            column_sum(cot[n] * mlp_out[n]),
+        ]
+        for n in each
+    ]
+    g_attn = join([(g_resid[n] * gate_a[n]).astype(BF16) for n in each])
     d_out[...] += dot(ctx_t, g_attn)
     d_outb[...] += column_sum(g_attn.astype(F32))
-    g_ctx = dot(g_attn, out_t[...]).astype(BF16)
-    gq_rows = []
-    g_keys = []
-    g_values = []
+    g_ctx = cut(dot(g_attn, out_t[...]).astype(BF16))
+    gq_rows = [[] for n in each]
+    g_keys = [[] for n in each]
+    g_values = [[] for n in each]
+    even = [None for n in each]
     for head in range(HEADS):
-        rows = slice(head * HEAD_DIM, (head + 1) * HEAD_DIM)
-        g_prob = dot_nt(half(pair(value, head), head), pair(g_ctx, head))
-        prob = probs[head]
-        g_score = (prob * (g_prob - column_sum(g_prob * prob))).astype(BF16)
-        gq_rows.append(dot(key_t[rows, :], g_score).astype(BF16))
-        g_key = dot(g_score, pair(query, head))
-        g_value = dot(probs_b[head], pair(g_ctx, head))
-        if head % 2 == 0:
-            even = (g_key, g_value)
-        else:
-            g_keys.append(jnp.where(low_half, even[0], g_key).astype(BF16))
-            g_values.append(jnp.where(low_half, even[1], g_value).astype(BF16))
-    g_query = jnp.concatenate(gq_rows, axis=0).T
-    g_qkv = jnp.concatenate([g_query] + g_keys + g_values, axis=1)
+        head_rows = slice(head * HEAD_DIM, (head + 1) * HEAD_DIM)
+        for n in each:
+            g_prob = dot_nt(half(pair(value[n], head), head), pair(g_ctx[n], head))
+            prob = probs[n][head]
+            g_score = (prob * (g_prob - column_sum(g_prob * prob))).astype(BF16)
+            gq_rows[n].append(dot(key_t[n][head_rows, :], g_score).astype(BF16))
+            g_key = dot(g_score, pair(query[n], head))
+            g_value = dot(probs_b[n][head], pair(g_ctx[n], head))
+            if head % 2 == 0:
+                even[n] = (g_key, g_value)
+            else:
+                g_keys[n].append(jnp.where(low_half, even[n][0], g_key).astype(BF16))
+                g_values[n].append(jnp.where(low_half, even[n][1], g_value).astype(BF16))
+    g_qkv = join(
+        [
+            jnp.concatenate([join(gq_rows[n]).T] + g_keys[n] + g_values[n], axis=1)
+            for n in each
+        ]
+    )
     d_qkv[...] += dot(hidden_a.T, g_qkv)
     d_qkvb[...] += column_sum(g_qkv.astype(F32))
-    g_hidden_a = dot(g_qkv, qkv_t[...])
-    g_shift_a = column_sum(g_hidden_a)
-    g_scale_a = column_sum(g_hidden_a * normed_a)
-    glat_ref[0] = (
-        g_resid + norm_back(g_hidden_a * (1.0 + scale_a), normed_a, inv_a)
-    ).astype(BF16)
-    gmod_ref[pl.ds(step, 1), :] = jnp.concatenate(
-        [g_shift_a, g_scale_a, g_gate_a, g_shift_m, g_scale_m, g_gate_m], axis=1
-    )
+    g_hidden_a = cut(dot(g_qkv, qkv_t[...]))
+    for n in each:
+        glat_ref[n] = (
+            g_resid[n] + norm_back(g_hidden_a[n] * (1.0 + scale_a[n]), normed_a[n], inv_a[n])
+        ).astype(BF16)
+        gmod_ref[pl.ds(step * PER + n, 1), :] = jnp.concatenate(
+            [column_sum(g_hidden_a[n]), column_sum(g_hidden_a[n] * normed_a[n])] + late_mod[n],
+            axis=1,
+        )
 
     @pl.when(step == steps - 1)
     def _():
@@ -290,35 +513,42 @@
             )
         put("fc2_b", d_fc2b)
         flat_ref[USED:tall, :] = jnp.zeros((tall - USED, LANE), F32)
-
-
-def run_block(latents, cotangent, condition, flat):
+        for owner in range(owners):
+            for lane, (first, last) in enumerate(spans):
+                block = flat_ref[owner * rows + first : owner * rows + last, :]
+                if last - first < half_rows:
+                    rest = jnp.zeros((half_rows - (last - first), LANE), F32)
+                    block = jnp.concatenate([block, rest], axis=0)
+                gpar_ref[lane, place_of(owner, orders[lane])] = block.astype(BF16)
+
+
+def run_block(latents, cotangent, condition, flat, rows):
     count = latents.shape[0]
-    tall = flat.shape[0]
     once = pl.Buffered(1)
-    latent_spec = pl.BlockSpec((1, SEQ, D), lambda i: (i, 0, 0))
+    latent_spec = pl.BlockSpec((PER, SEQ, D), lambda i: (i, 0, 0))
     return pl.pallas_call(
-        partial(block_kernel, count),
-        grid=(count,),
+        partial(block_kernel, count // PER, rows),
+        grid=(count // PER,),
         in_specs=[
             latent_spec,
             latent_spec,
             pl.BlockSpec((count, D), lambda i: (0, 0), pipeline_mode=once),
-            pl.BlockSpec((tall, LANE), lambda i: (0, 0), pipeline_mode=once),
+            pl.BlockSpec(flat.shape, lambda i: (0, 0, 0, 0), pipeline_mode=once),
         ],
         out_specs=[
             latent_spec,
             latent_spec,
             pl.BlockSpec((count, D), lambda i: (0, 0), pipeline_mode=once),
-            pl.BlockSpec((tall, LANE), lambda i: (0, 0), pipeline_mode=once),
+            pl.BlockSpec(flat.shape, lambda i: (0, 0, 0, 0), pipeline_mode=once),
         ],
         out_shape=[
             jax.ShapeDtypeStruct(latents.shape, BF16),
             jax.ShapeDtypeStruct(latents.shape, BF16),
             jax.ShapeDtypeStruct((count, D), F32),
-            jax.ShapeDtypeStruct((tall, LANE), F32),
+            jax.ShapeDtypeStruct(flat.shape, BF16),
         ],
         scratch_shapes=[
+            pltpu.VMEM((flat.shape[1] * rows, LANE), F32),
             pltpu.VMEM((D, 6 * D), BF16),
             pltpu.VMEM((D, 3 * D), BF16),
             pltpu.VMEM((D, D), BF16),
@@ -347,7 +577,11 @@
 
 
 def on_device(latents_in, class_ids, step_ids, class_table, step_table, params, cotangent):
-    flat = lax.all_gather(params.reshape(-1, LANE), "dp", axis=0, tiled=True)
+    devices = lax.axis_size("dp")
+    rows = params.shape[0] // LANE
+    half_rows = -(-rows // 32) * 16
+    mine = jnp.pad(params.reshape(rows, LANE), ((0, 2 * half_rows - rows), (0, 0)))
+    flat = gather(mine.reshape(2, half_rows, LANE), devices)
     class_hot = (
         class_ids[:, None] == jnp.arange(class_table.shape[0], dtype=jnp.int32)[None, :]
     ).astype(BF16)
@@ -356,9 +590,9 @@
     ).astype(BF16)
     condition = dot(class_hot, class_table) + dot(step_hot, step_table)
     block_out, grad_latents, grad_condition, grad_flat = run_block(
-        latents_in, cotangent, condition, flat
+        latents_in, cotangent, condition, flat, rows
     )
-    grad_params = lax.psum_scatter(grad_flat, "dp", scatter_dimension=0, tiled=True)
+    grad_params = reduce(grad_flat).reshape(2 * half_rows, LANE)[:rows]
     return block_out, grad_latents, grad_condition, grad_params.reshape(-1)
 
 

time: 389 us -> 252 us (0.65); the launches traced: 384 us -> 252 us
  blocking collectives: 120 us -> 0 us
  Pallas kernels: 166 us -> 241 us
  waiting for transfers between devices: 69.8 us -> 0 us
  between operations: 14.1 us -> 0.69 us
    unnamed x1 -> x0, blocking collectives: 120 us -> none
    pallas_call x1 -> x3, Pallas kernels: 166 us -> 241 us  [the longest x1 145 us: run_block(): pl.pallas_call(partial(block_kernel, count // PER, rows), grid=(count //...]
    all_gather x1 -> x0, waiting for transfers between devices: 68.2 us -> none  [on_device(): flat = lax.all_gather(params.reshape(-1, LANE), 'dp', axis=0, tiled=True)]
    unnamed x5 -> x6, local copies, waits for them, and re-layouts: 8.94 us -> 6.06 us
  transfers between devices with their start and end apart: 2 -> 0, of which waited for: 2 -> 0; matrix products, arithmetic and copies ran while one was open for 1% -> 0% of each run, Pallas kernels for 0% -> 0%
where the time goes in v2:
time: 252 us
  Pallas kernels  241 us (96%)
  local copies, waits for them, and re-layouts  7.74 us (3%)
  matrix products  2.94 us (1%)
    pallas_call x1, Pallas kernels, run_block(): pl.pallas_call(partial(block_kernel, count // PER, rows), grid=(count //...  145 us
    pallas_call x1, Pallas kernels, gather(): pl.pallas_call(partial(gather_kernel, count), in_specs=[pl.BlockSpec(memo...  49.6 us
    pallas_call x1, Pallas kernels, reduce(): pl.pallas_call(partial(reduce_kernel, count), in_specs=[pl.BlockSpec(memo...  46.5 us
    unnamed x6, local copies, waits for them, and re-layouts  6.06 us

profile of v2, /device:TPU:0, one launch (start us, length us, event | category | flops | bytes accessed | tf_op | source)
XLA Modules:
  0.0 252.1 jit_solution(5418201699860547415)
XLA Ops:
  0.6 0.0 copy-start
  0.6 1.1 copy-done
  1.8 0.9 fusion
  2.7 2.0 convolution_add_fusion.cond_ref
  4.7 0.9 pad.4
  5.6 49.6 %shard_map.102.par_ref = bf16[2,32,336,128]{3,2,1,0:T(8,128)(2,1)S(1)} custom-call(bf16[2,336,128]{2,1,0:T(8,128)(2,1)S(1)} %bitcast.8), custom_call_target="tpu_custom_call" | custom-call | tf_op jit(solution)/shard_map/pallas_call | solution.py:135
  55.2 0.0 copy-start.1
  55.2 2.4 copy-done.1
  57.6 144.7 %shard_map.103 = (bf16[16,256,384]{2,1,0:T(8,128)(2,1)}, bf16[16,256,384]{2,1,0:T(8,128)(2,1)}, f32[16,384]{1,0:T(8,128)}, bf16[2,32,336,128]{3,2,1,0:T(8,128)(2,1)}) custom-call(bf16[16,256,384]{2,1,0:T(8,128)(2,1)} %lat_ref.1, bf16[16,256,384]{2,1,0:T(8,128)(2,1)} %cot_ref.1, f32[16,384]{1,0:T(8,128)} %convolution_add_fusion.cond_ref, ...), custom_call_target="tpu_custom_call" | custom-call | tf_op jit(solution)/shard_map/pallas_call | solution.py:529
  202.3 0.0 copy-start.2
  202.3 2.6 %copy-done.2 = bf16[2,32,336,128]{3,2,1,0:T(8,128)(2,1)S(1)} copy-done((bf16[2,32,336,128]{3,2,1,0:T(8,128)(2,1)S(1)}, bf16[2,32,336,128]{3,2,1,0:T(8,128)(2,1)}, u32[]{:S(2)}) %copy-start.2) | copy-done | bytes 5505048
  204.8 46.5 %shard_map.104 = f32[2,336,128]{2,1,0:T(8,128)S(1)} custom-call(bf16[2,32,336,128]{3,2,1,0:T(8,128)(2,1)S(1)} %copy-done.2), custom_call_target="tpu_custom_call" | custom-call | tf_op jit(solution)/shard_map/pallas_call | solution.py:211
  251.4 0.7 slice_bitcast_fusion
Async XLA Ops:
  0.6 1.1 copy-start
  55.2 2.4 copy-start.1
  202.3 2.6 %copy-start.2 = (bf16[2,32,336,128]{3,2,1,0:T(8,128)(2,1)S(1)}, bf16[2,32,336,128]{3,2,1,0:T(8,128)(2,1)}, u32[]{:S(2)}) copy-start(bf16[2,32,336,128]{3,2,1,0:T(8,128)(2,1)} %get-tuple-element.11.all_ref) | copy-start | bytes 16515076

commit v3 on v2

--- a/solution.py
+++ b/solution.py
@@ -160,10 +160,7 @@
     def start(lane, stage):
         size = count // 2 ** (stage + 1)
         side = places[lane] // size % 2
-        if stage == 0:
-            source = all_ref.at[lane, pl.ds((1 - side) * size, size)]
-        else:
-            source = land_ref.at[lane, pl.ds(2 * size + (1 - side) * size, size)]
+        source = land_ref.at[lane, pl.ds(2 * size + (1 - side) * size, size)]
         copy = pltpu.make_async_remote_copy(
             src_ref=source,
             dst_ref=land_ref.at[lane, pl.ds(size, size)],
@@ -180,10 +177,7 @@
         side = places[lane] // size % 2
 
         def one(block):
-            if stage == 0:
-                kept = all_ref[lane, side * size + block]
-            else:
-                kept = land_ref[lane, 2 * size + side * size + block]
+            kept = land_ref[lane, 2 * size + side * size + block]
             return kept.astype(F32) + land_ref[lane, size + block].astype(F32)
 
         if stage == bits - 1:
@@ -196,8 +190,48 @@
 
             lax.fori_loop(0, size, body, 0)
 
-    flying = [start(lane, 0) for lane in range(2)]
-    for stage in range(bits):
+    quarter = count // 4
+
+    def first_place(lane, piece):
+        side = places[lane] // quarter % 2
+        return (1 - side if piece == 0 else side) * quarter
+
+    def first_start(lane, piece):
+        side = places[lane] // (2 * quarter) % 2
+        offset = first_place(lane, piece)
+        copy = pltpu.make_async_remote_copy(
+            src_ref=all_ref.at[lane, pl.ds((1 - side) * 2 * quarter + offset, quarter)],
+            dst_ref=land_ref.at[lane, pl.ds(2 * quarter + offset, quarter)],
+            send_sem=send_sem.at[lane, piece * bits],
+            recv_sem=recv_sem.at[lane, piece * bits],
+            device_id=(partner_of(me, orders[lane][0]),),
+            device_id_type=pl.DeviceIdType.MESH,
+        )
+        copy.start()
+        return copy
+
+    def first_add(lane, piece):
+        side = places[lane] // (2 * quarter) % 2
+        offset = first_place(lane, piece)
+
+        def body(block, carry):
+            kept = all_ref[lane, side * 2 * quarter + offset + block].astype(F32)
+            there = 2 * quarter + offset + block
+            land_ref[lane, there] = (kept + land_ref[lane, there].astype(F32)).astype(BF16)
+            return carry
+
+        lax.fori_loop(0, quarter, body, 0)
+
+    opening = [[first_start(lane, piece) for lane in range(2)] for piece in range(2)]
+    flying = [None, None]
+    for lane in range(2):
+        opening[0][lane].wait()
+        first_add(lane, 0)
+        flying[lane] = start(lane, 1)
+    for lane in range(2):
+        opening[1][lane].wait()
+        first_add(lane, 1)
+    for stage in range(1, bits):
         for lane in range(2):
             flying[lane].wait()
             add(lane, stage)
@@ -215,8 +249,8 @@
         out_shape=jax.ShapeDtypeStruct((lanes, half, width), F32),
         scratch_shapes=[
             pltpu.VMEM((lanes, count, half, width), BF16),
-            pltpu.SemaphoreType.DMA((2, bits)),
-            pltpu.SemaphoreType.DMA((2, bits)),
+            pltpu.SemaphoreType.DMA((2, bits + 1)),
+            pltpu.SemaphoreType.DMA((2, bits + 1)),
         ],
         compiler_params=pltpu.CompilerParams(
             collective_id=1, has_side_effects=True, vmem_limit_bytes=40 * 1024 * 1024

time: 252 us -> 250 us (level)
  no operation moved by 1% of the time
where the time goes in v3:
time: 250 us
  Pallas kernels  239 us (96%)
  local copies, waits for them, and re-layouts  7.74 us (3%)
  matrix products  2.94 us (1%)
    pallas_call x1, Pallas kernels, run_block(): pl.pallas_call(partial(block_kernel, count // PER, rows), grid=(count //...  145 us
    pallas_call x1, Pallas kernels, gather(): pl.pallas_call(partial(gather_kernel, count), in_specs=[pl.BlockSpec(memo...  49.6 us
    pallas_call x1, Pallas kernels, reduce(): pl.pallas_call(partial(reduce_kernel, count), in_specs=[pl.BlockSpec(memo...  44.5 us
    unnamed x6, local copies, waits for them, and re-layouts  6.06 us

profile of v3, /device:TPU:0, one launch (start us, length us, event | category | flops | bytes accessed | tf_op | source)
XLA Modules:
  0.0 250.1 jit_solution(42260729459870281)
XLA Ops:
  0.6 0.0 copy-start
  0.6 1.1 copy-done
  1.8 0.9 fusion
  2.7 2.0 convolution_add_fusion.cond_ref
  4.7 0.9 pad.4
  5.6 49.6 %shard_map.102.par_ref = bf16[2,32,336,128]{3,2,1,0:T(8,128)(2,1)S(1)} custom-call(bf16[2,336,128]{2,1,0:T(8,128)(2,1)S(1)} %bitcast.8), custom_call_target="tpu_custom_call" | custom-call | tf_op jit(solution)/shard_map/pallas_call | solution.py:135
  55.2 0.0 copy-start.1
  55.2 2.4 copy-done.1
  57.6 144.7 %shard_map.103 = (bf16[16,256,384]{2,1,0:T(8,128)(2,1)}, bf16[16,256,384]{2,1,0:T(8,128)(2,1)}, f32[16,384]{1,0:T(8,128)}, bf16[2,32,336,128]{3,2,1,0:T(8,128)(2,1)}) custom-call(bf16[16,256,384]{2,1,0:T(8,128)(2,1)} %lat_ref.1, bf16[16,256,384]{2,1,0:T(8,128)(2,1)} %cot_ref.1, f32[16,384]{1,0:T(8,128)} %convolution_add_fusion.cond_ref, ...), custom_call_target="tpu_custom_call" | custom-call | tf_op jit(solution)/shard_map/pallas_call | solution.py:563
  202.3 0.0 copy-start.2
  202.3 2.6 %copy-done.2 = bf16[2,32,336,128]{3,2,1,0:T(8,128)(2,1)S(1)} copy-done((bf16[2,32,336,128]{3,2,1,0:T(8,128)(2,1)S(1)}, bf16[2,32,336,128]{3,2,1,0:T(8,128)(2,1)}, u32[]{:S(2)}) %copy-start.2) | copy-done | bytes 5505048
  204.8 44.5 %shard_map.104 = f32[2,336,128]{2,1,0:T(8,128)S(1)} custom-call(bf16[2,32,336,128]{3,2,1,0:T(8,128)(2,1)S(1)} %copy-done.2), custom_call_target="tpu_custom_call" | custom-call | tf_op jit(solution)/shard_map/pallas_call | solution.py:245
  249.4 0.7 slice_bitcast_fusion
Async XLA Ops:
  0.6 1.1 copy-start
  55.2 2.4 copy-start.1
  202.3 2.6 %copy-start.2 = (bf16[2,32,336,128]{3,2,1,0:T(8,128)(2,1)S(1)}, bf16[2,32,336,128]{3,2,1,0:T(8,128)(2,1)}, u32[]{:S(2)}) copy-start(bf16[2,32,336,128]{3,2,1,0:T(8,128)(2,1)} %get-tuple-element.11.all_ref) | copy-start | bytes 16515076
